TPU v7x, 512 devices: a whole 4x4x16 slice. The times are simulated.
512 devices in a mesh: brow: 16 (over z), bcol: 32 (over y, x, core).
Axes of the slice: x: 4, y: 4, z: 16, core: 2. Of those that a mesh axis runs over, the one named last changes fastest.
Arguments:
- ancestor_cov: bfloat16 [5632, 5632], P('brow', 'bcol'), may hold values from -1 to 4
- ancestor_pattern: int32 [22], replicated, may hold values 0 or 1
- parent_panel: bfloat16 [5632, 4096], P('brow'), may hold values from -0.5 to 0.5
- parent_inverse: bfloat16 [4096, 4096], P('brow', 'bcol'), may hold values from -1 to 4
- child_pattern: int32 [16], replicated, may hold values 0 or 1
- child_panel: bfloat16 [4096, 4096], P('brow', 'bcol'), may hold values from -0.3125 to 0.3125
- child_inverse: bfloat16 [4096, 4096], P('brow', 'bcol'), may hold values from -1 to 4
Outputs:
- ancestor_block: bfloat16 [5632, 4096], P('brow', 'bcol')
- parent_diag: bfloat16 [4096, 4096], P('brow', 'bcol')
- parent_child: bfloat16 [4096, 4096], P('brow', 'bcol')
- child_diag: bfloat16 [4096, 4096], P('brow', 'bcol')
All inputs are finite; a program needn't handle non-finite values.
Results may differ from a plain program's by a relative error of at most 0.006.
Values may be sent and summed in bfloat16 or wider, within the bound.
No kernel may reach another device: no remote copies, remote signals or barrier semaphores. Data moves between devices by JAX's collectives and lax.ppermute only.
A program may use at most 64 MiB of HBM per device.

v0:
```python
import jax
import jax.numpy as jnp
from jax import lax
from jax.sharding import PartitionSpec as P


def block_keep(pattern, first_row, count, total_rows):
    block_rows = total_rows // pattern.shape[0]
    row_ids = first_row + lax.iota(jnp.int32, count)
    block_ids = lax.iota(jnp.int32, pattern.shape[0])
    matches = row_ids[:, None] // block_rows == block_ids[None, :]
    return jnp.sum(jnp.where(matches, pattern[None, :], 0), axis=1)


def per_device(
    ancestor_cov,
    ancestor_pattern,
    parent_panel,
    parent_inverse,
    child_pattern,
    child_panel,
    child_inverse,
):
    row_index = lax.axis_index("brow")
    column_index = lax.axis_index("bcol")
    row_devices = lax.axis_size("brow")
    local_rows = parent_panel.shape[0]
    band_rows = parent_inverse.shape[0]
    band_columns = parent_inverse.shape[1]
    ancestor_keep = block_keep(
        ancestor_pattern, row_index * local_rows, local_rows, local_rows * row_devices
    )
    child_keep = block_keep(
        child_pattern, row_index * band_rows, band_rows, band_rows * row_devices
    )
    parent_masked = parent_panel * ancestor_keep[:, None].astype(jnp.bfloat16)
    child_masked = child_panel * child_keep[:, None].astype(jnp.bfloat16)
    panel_slab = lax.dynamic_slice_in_dim(
        parent_masked, column_index * band_columns, band_columns, 1
    )
    parent_columns, child_columns = (
        lax.all_gather(panel_slab, "brow", axis=0, tiled=True),
        lax.all_gather(child_masked, "brow", axis=0, tiled=True),
    )
    factor_rows = parent_columns
    ancestor_sum = jnp.dot(
        lax.all_gather(ancestor_cov, "bcol", axis=1, tiled=True),
        factor_rows,
        preferred_element_type=jnp.float32,
    )
    ancestor_block = (-ancestor_sum * ancestor_keep[:, None].astype(jnp.float32)).astype(
        jnp.bfloat16
    )
    parent_wide = lax.all_to_all(parent_masked, "brow", split_axis=1, concat_axis=0, tiled=True)
    image_band = lax.all_gather(ancestor_block, "brow", axis=0, tiled=True)
    parent_inner = jnp.einsum(
        "ka,kb->ab", parent_wide, image_band, preferred_element_type=jnp.float32
    )
    parent_diag = (parent_inverse.astype(jnp.float32) - parent_inner).astype(jnp.bfloat16)
    factor_rows = child_columns
    parent_sum = jnp.dot(
        lax.all_gather(parent_diag, "bcol", axis=1, tiled=True),
        factor_rows,
        preferred_element_type=jnp.float32,
    )
    parent_child = (-parent_sum * child_keep[:, None].astype(jnp.float32)).astype(jnp.bfloat16)
    child_band = lax.all_gather(child_masked, "bcol", axis=1, tiled=True)
    child_inner = lax.psum_scatter(
        jnp.einsum("ka,kb->ab", child_band, parent_child, preferred_element_type=jnp.float32),
        "brow",
        scatter_dimension=0,
        tiled=True,
    )
    child_diag = (child_inverse.astype(jnp.float32) - child_inner).astype(jnp.bfloat16)
    return (ancestor_block, parent_diag, parent_child, child_diag)


def solution(mesh):
    return jax.shard_map(
        per_device,
        mesh=mesh,
        in_specs=(
            P("brow", "bcol"),
            P(),
            P("brow", None),
            P("brow", "bcol"),
            P(),
            P("brow", "bcol"),
            P("brow", "bcol"),
        ),
        out_specs=(P("brow", "bcol"), P("brow", "bcol"), P("brow", "bcol"), P("brow", "bcol")),
        check_vma=False,
    )
```

profile of v0, /device:TPU:8, one launch (start us, length us, event | category | flops | bytes accessed | tf_op | source)
XLA Modules:
  0.0 577.8 jit_solution(14311863399539205714)
XLA Ops:
  7.2 0.0 all-gather.7.cloned.1.call-start
  7.2 0.7 select_reduce_fusion
  8.0 2.1 broadcast_multiply_fusion
  10.1 0.7 constant_dynamic-slice_fusion
  10.7 0.0 all-gather.7.cloned.1.call-update
  10.8 0.0 all-gather.9.cloned.1.call-start
  10.8 0.7 all-gather.9.cloned.1.call-update
  11.5 1.9 copy.16
  13.4 15.2 %all-to-all-start = ((bf16[352,16,256]{2,0,1:T(8,128)(2,1)}), bf16[352,16,256]{2,0,1:T(8,128)(2,1)S(1)}, u32[]{:S(2)}, u32[]{:S(2)}) async-start(bf16[352,16,256]{2,0,1:T(8,128)(2,1)} %bitcast.19), calls=%async_computation | async-start | bytes 5767168 | tf_op jit(solution)/shard_map/all_to_all | solution.py:54
  28.6 0.0 all-gather.11.cloned.1.call-start
  28.7 119.7 %all-gather.7.cloned.1.call-done = bf16[5632,128]{1,0:T(8,128)(2,1)} async-done(((bf16[352,128]{1,0:T(8,128)(2,1)}), bf16[5632,128]{1,0:T(8,128)(2,1)}) %all-gather.7.cloned.1.call-update) | async-done | bytes 1441808 | tf_op jit(solution)/shard_map/all_gather | solution.py:42
  148.3 73.0 %all-gather.9.cloned.1.call-done = bf16[352,5632]{0,1:T(8,128)(2,1)} async-done(((bf16[352,176]{0,1:T(8,128)(2,1)}), bf16[352,5632]{0,1:T(8,128)(2,1)}) %all-gather.9.cloned.1.call-update) | async-done | bytes 3964944 | tf_op jit(solution)/shard_map/all_gather | solution.py:47
  221.3 0.0 copy-start.4
  221.3 0.0 copy-start.2
  221.3 0.0 copy-start.1
  221.3 5.1 fusion.5
  226.4 0.0 all-gather.11.cloned.1.call-update
  226.4 0.0 all-gather.15.cloned.1.call-start
  226.5 0.0 copy-done.4
  226.5 0.1 select_reduce_fusion.1
  226.6 0.0 copy-done.2
  226.6 0.7 broadcast_multiply_fusion.1
  227.3 0.0 all-gather.15.cloned.1.call-update
  227.4 0.0 all-gather.13.cloned.1.call-start
  227.4 71.0 %all-gather.11.cloned.1.call-done = bf16[5632,128]{1,0:T(8,128)(2,1)} async-done(((bf16[352,128]{1,0:T(8,128)(2,1)}), bf16[5632,128]{1,0:T(8,128)(2,1)}) %all-gather.11.cloned.1.call-update) | async-done | bytes 1441808 | tf_op jit(solution)/shard_map/all_gather | solution.py:55
  298.4 0.0 all-to-all-done
  298.4 0.0 copy-done.1
  298.4 2.9 fusion.3
  301.4 0.0 all-gather.13.cloned.1.call-update
  301.4 0.0 all-gather.17.cloned.1.call-start
  301.4 0.5 all-gather.17.cloned.1.call-update
  302.0 0.0 reduce-scatter.2.cloned.1.call-start
  302.0 66.9 %all-gather.15.cloned.1.call-done = bf16[4096,128]{1,0:T(8,128)(2,1)} async-done(((bf16[256,128]{1,0:T(8,128)(2,1)}), bf16[4096,128]{1,0:T(8,128)(2,1)}) %all-gather.15.cloned.1.call-update) | async-done | bytes 1048592 | tf_op jit(solution)/shard_map/all_gather | solution.py:43
  368.9 60.1 %all-gather.13.cloned.1.call-done = bf16[256,4096]{1,0:T(8,128)(2,1)} async-done(((bf16[256,128]{1,0:T(8,128)(2,1)}), bf16[256,4096]{1,0:T(8,128)(2,1)}) %all-gather.13.cloned.1.call-update) | async-done | bytes 2097168 | tf_op jit(solution)/shard_map/all_gather | solution.py:62
  429.0 2.6 fusion.4
  431.6 0.0 copy-start
  431.6 60.5 %all-gather.17.cloned.1.call-done = bf16[256,4096]{1,0:T(8,128)(2,1)} async-done(((bf16[256,128]{1,0:T(8,128)(2,1)}), bf16[256,4096]{1,0:T(8,128)(2,1)}) %all-gather.17.cloned.1.call-update) | async-done | bytes 2097168 | tf_op jit(solution)/shard_map/all_gather | solution.py:67
  492.2 3.7 fusion.11
  495.8 0.0 copy-done
  495.8 0.0 copy-start.3
  495.8 0.0 reduce-scatter.2.cloned.1.call-update
  495.8 73.5 %reduce-scatter.2.cloned.1.call-done = f32[256,128]{1,0:T(8,128)} async-done(((f32[4096,128]{1,0:T(8,128)}), f32[256,128]{1,0:T(8,128)}) %reduce-scatter.2.cloned.1.call-update) | async-done | bytes 131088 | tf_op jit(solution)/shard_map/reduce_scatter | solution.py:68
  569.4 0.0 copy-done.3
  569.4 1.5 subtract_convert_fusion
  (4 shorter events, 0.0 us)
Async XLA Ops:
  7.2 141.2 %all-gather.7.cloned.1.call-start = ((), (), s32[]{:S(2)}) async-start(), calls=%async_computation.2 | async-start | bytes 1531904 | tf_op jit(solution)/shard_map/all_gather | solution.py:42
  10.8 210.5 %all-gather.9.cloned.1.call-start = ((), (), s32[]{:S(2)}) async-start(), calls=%async_computation.3 | async-start | bytes 4460544 | tf_op jit(solution)/shard_map/all_gather | solution.py:47
  13.4 285.0 %all-to-all-start = ((bf16[352,16,256]{2,0,1:T(8,128)(2,1)}), bf16[352,16,256]{2,0,1:T(8,128)(2,1)S(1)}, u32[]{:S(2)}, u32[]{:S(2)}) async-start(bf16[352,16,256]{2,0,1:T(8,128)(2,1)} %bitcast.19), calls=%async_computation | async-start | bytes 5767168 | tf_op jit(solution)/shard_map/all_to_all | solution.py:54
  28.6 269.8 %all-gather.11.cloned.1.call-start = ((), (), s32[]{:S(2)}) async-start(), calls=%async_computation.4 | async-start | bytes 1531904 | tf_op jit(solution)/shard_map/all_gather | solution.py:55
  221.3 5.2 copy-start.4
  221.3 5.3 copy-start.2
  221.3 77.1 %copy-start.1 = (bf16[256,128]{1,0:T(8,128)(2,1)S(1)}, bf16[256,128]{1,0:T(8,128)(2,1)}, u32[]{:S(2)}) copy-start(bf16[256,128]{1,0:T(8,128)(2,1)} %param.10) | copy-start | bytes 196612
  226.4 142.5 %all-gather.15.cloned.1.call-start = ((), (), s32[]{:S(2)}) async-start(), calls=%async_computation.6 | async-start | bytes 1114112 | tf_op jit(solution)/shard_map/all_gather | solution.py:43
  227.4 201.7 %all-gather.13.cloned.1.call-start = ((), (), s32[]{:S(2)}) async-start(), calls=%async_computation.5 | async-start | bytes 2162688 | tf_op jit(solution)/shard_map/all_gather | solution.py:62
  301.4 190.8 %all-gather.17.cloned.1.call-start = ((), (), s32[]{:S(2)}) async-start(), calls=%async_computation.7 | async-start | bytes 2162688 | tf_op jit(solution)/shard_map/all_gather | solution.py:67
  302.0 267.4 %reduce-scatter.2.cloned.1.call-start = ((), (), s32[]{:S(2)}) async-start(), calls=%async_computation.8 | async-start | bytes 2228224 | tf_op jit(solution)/shard_map/reduce_scatter | solution.py:68
  431.6 64.2 %copy-start = (bf16[256,128]{1,0:T(8,128)(2,1)}, bf16[256,128]{1,0:T(8,128)(2,1)S(1)}, u32[]{:S(2)}) copy-start(bf16[256,128]{1,0:T(8,128)(2,1)S(1)} %fusion.4) | copy-start | bytes 196612
  495.8 73.6 %copy-start.3 = (bf16[256,128]{1,0:T(8,128)(2,1)S(1)}, bf16[256,128]{1,0:T(8,128)(2,1)}, u32[]{:S(2)}) copy-start(bf16[256,128]{1,0:T(8,128)(2,1)} %param.13) | copy-start | bytes 196612
Sparse Core Ops, SparseCore 0:
  10.9 137.3 all-gather.6
  151.5 69.7 all-gather.8
  226.5 71.8 all-gather.10
  300.9 67.9 all-gather.14
  372.4 56.5 all-gather.12
  432.5 59.5 all-gather.16
  496.0 73.3 reduce-scatter.1
where the time goes:
time: 578 us
  waiting for transfers between devices  526 us (91%)
  starting transfers between devices  15.5 us (3%)
  matrix products  14.2 us (2%)
  between operations  14.2 us (2%)
    all_gather x1, waiting for transfers between devices, per_device(): lax.all_gather(panel_slab, 'brow', axis=0, tiled=True)  120 us
    reduce_scatter x1, waiting for transfers between devices, per_device(): lax.psum_scatter(jnp.einsum('ka,kb->ab', child_band, parent_child, prefer...  73.5 us
    all_gather x1, waiting for transfers between devices, per_device(): lax.all_gather(ancestor_cov, 'bcol', axis=1, tiled=True)  73 us
    all_gather x1, waiting for transfers between devices, per_device(): image_band = lax.all_gather(ancestor_block, 'brow', axis=0, tiled=True)  71 us
    all_gather x1, waiting for transfers between devices, per_device(): lax.all_gather(child_masked, 'brow', axis=0, tiled=True)  66.9 us
    all_gather x1, waiting for transfers between devices, per_device(): child_band = lax.all_gather(child_masked, 'bcol', axis=1, tiled=True)  60.5 us
    all_gather x1, waiting for transfers between devices, per_device(): lax.all_gather(parent_diag, 'bcol', axis=1, tiled=True)  60.1 us
    all_to_all x1, starting transfers between devices, per_device(): lax.all_to_all(parent_masked, 'brow', split_axis=1, concat_axis=0, tiled=...  15.2 us
  transfers between devices with their start and end apart: 8, of which 7 were waited for; matrix products, arithmetic and copies ran while one was open for 2% of the time, Pallas kernels for 0%

commit v1 on v0

--- a/solution.py
+++ b/solution.py
@@ -40,7 +40,9 @@
     )
     parent_columns, child_columns = (
         lax.all_gather(panel_slab, "brow", axis=0, tiled=True),
-        lax.all_gather(child_masked, "brow", axis=0, tiled=True),
+        jnp.concatenate(
+            lax.all_to_all(jnp.stack([child_masked] * lax.axis_size("brow")), "brow", 0, 0), axis=0
+        ),
     )
     factor_rows = parent_columns
     ancestor_sum = jnp.dot(

time: 578 us -> 513 us (0.89)
  the two profiles are of different devices: /device:TPU:8 before, /device:TPU:4 now
where the time goes in v1:
time: 513 us
  waiting for transfers between devices  453 us (88%)
  starting transfers between devices  23.4 us (5%)
  between operations  14.2 us (3%)
  matrix products  14 us (3%)
    all_gather x1, waiting for transfers between devices, per_device(): lax.all_gather(panel_slab, 'brow', axis=0, tiled=True)  128 us
    reduce_scatter x1, waiting for transfers between devices, per_device(): lax.psum_scatter(jnp.einsum('ka,kb->ab', child_band, parent_child, prefer...  74.6 us
    all_gather x1, waiting for transfers between devices, per_device(): image_band = lax.all_gather(ancestor_block, 'brow', axis=0, tiled=True)  72.3 us
    all_gather x1, waiting for transfers between devices, per_device(): lax.all_gather(ancestor_cov, 'bcol', axis=1, tiled=True)  70.2 us
    all_gather x1, waiting for transfers between devices, per_device(): child_band = lax.all_gather(child_masked, 'bcol', axis=1, tiled=True)  60.8 us
    all_to_all x1, waiting for transfers between devices, per_device(): lax.all_to_all(jnp.stack([child_masked] * lax.axis_size('brow')), 'brow',...  38.7 us
    all_to_all x1, starting transfers between devices, per_device(): lax.all_to_all(parent_masked, 'brow', split_axis=1, concat_axis=0, tiled=...  15.2 us
  transfers between devices with their start and end apart: 8, of which 7 were waited for; matrix products, arithmetic and copies ran while one was open for 2% of the time, Pallas kernels for 0%

profile of v1, /device:TPU:4, one launch (start us, length us, event | category | flops | bytes accessed | tf_op | source)
XLA Modules:
  0.0 512.9 jit_solution(4215735119368795318)
XLA Ops:
  7.2 0.0 all-gather.6.cloned.1.call-start
  7.2 0.7 select_reduce_fusion
  8.0 2.1 broadcast_multiply_fusion
  10.1 0.7 constant_dynamic-slice_fusion
  10.7 0.0 all-gather.6.cloned.1.call-update
  10.8 1.9 copy.16
  12.7 15.2 %all-to-all-start = ((bf16[352,16,256]{2,0,1:T(8,128)(2,1)}), bf16[352,16,256]{2,0,1:T(8,128)(2,1)S(1)}, u32[]{:S(2)}, u32[]{:S(2)}) async-start(bf16[352,16,256]{2,0,1:T(8,128)(2,1)} %bitcast.20), calls=%async_computation | async-start | bytes 5767168 | tf_op jit(solution)/shard_map/all_to_all | solution.py:56
  27.9 0.0 all-gather.8.cloned.1.call-start
  27.9 0.7 all-gather.8.cloned.1.call-update
  28.6 0.0 all-gather.10.cloned.1.call-start
  28.7 127.8 %all-gather.6.cloned.1.call-done = bf16[5632,128]{1,0:T(8,128)(2,1)} async-done(((bf16[352,128]{1,0:T(8,128)(2,1)}), bf16[5632,128]{1,0:T(8,128)(2,1)}) %all-gather.6.cloned.1.call-update) | async-done | bytes 1441808 | tf_op jit(solution)/shard_map/all_gather | solution.py:42
  156.4 70.2 %all-gather.8.cloned.1.call-done = bf16[352,5632]{0,1:T(8,128)(2,1)} async-done(((bf16[352,176]{0,1:T(8,128)(2,1)}), bf16[352,5632]{0,1:T(8,128)(2,1)}) %all-gather.8.cloned.1.call-update) | async-done | bytes 3964944 | tf_op jit(solution)/shard_map/all_gather | solution.py:49
  226.6 0.0 copy-start.2
  226.7 5.1 fusion.5
  231.7 0.0 all-gather.10.cloned.1.call-update
  231.8 0.0 all-gather.12.cloned.1.call-start
  231.8 72.3 %all-gather.10.cloned.1.call-done = bf16[5632,128]{1,0:T(8,128)(2,1)} async-done(((bf16[352,128]{1,0:T(8,128)(2,1)}), bf16[5632,128]{1,0:T(8,128)(2,1)}) %all-gather.10.cloned.1.call-update) | async-done | bytes 1441808 | tf_op jit(solution)/shard_map/all_gather | solution.py:57
  304.1 0.0 all-to-all-done
  304.1 0.0 copy-done.2
  304.1 0.0 copy-start.5
  304.1 0.0 copy-start.3
  304.1 3.0 fusion.3
  307.1 0.0 all-gather.12.cloned.1.call-update
  307.1 0.0 copy-done.5
  307.1 0.1 select_reduce_fusion.1
  307.2 0.0 copy-done.3
  307.2 0.1 broadcast_multiply_fusion.1
  307.3 0.0 copy-start
  307.3 1.2 stack.2
  308.5 7.9 %all-to-all-start.1 = ((bf16[16,256,128]{2,1,0:T(8,128)(2,1)}), bf16[16,256,128]{2,1,0:T(8,128)(2,1)S(1)}, u32[]{:S(2)}, u32[]{:S(2)}) async-start(bf16[16,256,128]{2,1,0:T(8,128)(2,1)} %stack.2), calls=%async_computation.1 | async-start | bytes 2097152 | tf_op jit(solution)/shard_map/all_to_all | solution.py:44
  316.4 0.0 all-gather.14.cloned.1.call-start
  316.5 0.0 copy-done
  316.5 0.5 all-gather.14.cloned.1.call-update
  317.0 0.0 reduce-scatter.2.cloned.1.call-start
  317.1 38.7 %all-to-all-done.1 = bf16[16,256,128]{2,1,0:T(8,128)(2,1)S(1)} async-done(((bf16[16,256,128]{2,1,0:T(8,128)(2,1)}), bf16[16,256,128]{2,1,0:T(8,128)(2,1)S(1)}, u32[]{:S(2)}, u32[]{:S(2)}) %all-to-all-start.1) | async-done | bytes 1048608 | tf_op jit(solution)/shard_map/all_to_all | solution.py:44
  355.8 7.3 %all-gather.12.cloned.1.call-done = bf16[256,4096]{1,0:T(8,128)(2,1)} async-done(((bf16[256,128]{1,0:T(8,128)(2,1)}), bf16[256,4096]{1,0:T(8,128)(2,1)}) %all-gather.12.cloned.1.call-update) | async-done | bytes 2097168 | tf_op jit(solution)/shard_map/all_gather | solution.py:64
  363.1 2.3 fusion.4
  365.4 0.0 copy-start.1
  365.4 60.8 %all-gather.14.cloned.1.call-done = bf16[256,4096]{1,0:T(8,128)(2,1)} async-done(((bf16[256,128]{1,0:T(8,128)(2,1)}), bf16[256,4096]{1,0:T(8,128)(2,1)}) %all-gather.14.cloned.1.call-update) | async-done | bytes 2097168 | tf_op jit(solution)/shard_map/all_gather | solution.py:69
  426.2 3.7 fusion.11
  429.9 0.0 copy-done.1
  429.9 0.0 copy-start.4
  429.9 0.0 reduce-scatter.2.cloned.1.call-update
  429.9 74.6 %reduce-scatter.2.cloned.1.call-done = f32[256,128]{1,0:T(8,128)} async-done(((f32[4096,128]{1,0:T(8,128)}), f32[256,128]{1,0:T(8,128)}) %reduce-scatter.2.cloned.1.call-update) | async-done | bytes 131088 | tf_op jit(solution)/shard_map/reduce_scatter | solution.py:70
  504.5 0.0 copy-done.4
  504.5 1.5 subtract_convert_fusion
  (4 shorter events, 0.0 us)
Async XLA Ops:
  7.2 149.3 %all-gather.6.cloned.1.call-start = ((), (), s32[]{:S(2)}) async-start(), calls=%async_computation.3 | async-start | bytes 1531904 | tf_op jit(solution)/shard_map/all_gather | solution.py:42
  12.7 291.4 %all-to-all-start = ((bf16[352,16,256]{2,0,1:T(8,128)(2,1)}), bf16[352,16,256]{2,0,1:T(8,128)(2,1)S(1)}, u32[]{:S(2)}, u32[]{:S(2)}) async-start(bf16[352,16,256]{2,0,1:T(8,128)(2,1)} %bitcast.20), calls=%async_computation | async-start | bytes 5767168 | tf_op jit(solution)/shard_map/all_to_all | solution.py:56
  27.9 198.8 %all-gather.8.cloned.1.call-start = ((), (), s32[]{:S(2)}) async-start(), calls=%async_computation.4 | async-start | bytes 4460544 | tf_op jit(solution)/shard_map/all_gather | solution.py:49
  28.6 275.4 %all-gather.10.cloned.1.call-start = ((), (), s32[]{:S(2)}) async-start(), calls=%async_computation.5 | async-start | bytes 1531904 | tf_op jit(solution)/shard_map/all_gather | solution.py:57
  226.6 77.4 %copy-start.2 = (bf16[256,128]{1,0:T(8,128)(2,1)S(1)}, bf16[256,128]{1,0:T(8,128)(2,1)}, u32[]{:S(2)}) copy-start(bf16[256,128]{1,0:T(8,128)(2,1)} %param.10) | copy-start | bytes 196612
  231.8 131.4 %all-gather.12.cloned.1.call-start = ((), (), s32[]{:S(2)}) async-start(), calls=%async_computation.6 | async-start | bytes 2162688 | tf_op jit(solution)/shard_map/all_gather | solution.py:64
  304.1 3.0 copy-start.5
  304.1 3.1 copy-start.3
  307.3 9.2 %copy-start = (bf16[256,128]{1,0:T(8,128)(2,1)}, bf16[256,128]{1,0:T(8,128)(2,1)S(1)}, u32[]{:S(2)}) copy-start(bf16[256,128]{1,0:T(8,128)(2,1)S(1)} %broadcast_multiply_fusion.1) | copy-start | bytes 196612
  308.5 47.3 %all-to-all-start.1 = ((bf16[16,256,128]{2,1,0:T(8,128)(2,1)}), bf16[16,256,128]{2,1,0:T(8,128)(2,1)S(1)}, u32[]{:S(2)}, u32[]{:S(2)}) async-start(bf16[16,256,128]{2,1,0:T(8,128)(2,1)} %stack.2), calls=%async_computation.1 | async-start | bytes 2097152 | tf_op jit(solution)/shard_map/all_to_all | solution.py:44
  316.4 109.8 %all-gather.14.cloned.1.call-start = ((), (), s32[]{:S(2)}) async-start(), calls=%async_computation.7 | async-start | bytes 2162688 | tf_op jit(solution)/shard_map/all_gather | solution.py:69
  317.0 187.5 %reduce-scatter.2.cloned.1.call-start = ((), (), s32[]{:S(2)}) async-start(), calls=%async_computation.8 | async-start | bytes 2228224 | tf_op jit(solution)/shard_map/reduce_scatter | solution.py:70
  365.4 64.5 %copy-start.1 = (bf16[256,128]{1,0:T(8,128)(2,1)}, bf16[256,128]{1,0:T(8,128)(2,1)S(1)}, u32[]{:S(2)}) copy-start(bf16[256,128]{1,0:T(8,128)(2,1)S(1)} %fusion.4) | copy-start | bytes 196612
  429.9 74.6 %copy-start.4 = (bf16[256,128]{1,0:T(8,128)(2,1)S(1)}, bf16[256,128]{1,0:T(8,128)(2,1)}, u32[]{:S(2)}) copy-start(bf16[256,128]{1,0:T(8,128)(2,1)} %param.13) | copy-start | bytes 196612
Sparse Core Ops, SparseCore 0:
  10.9 145.4 all-gather.5
  159.6 66.9 all-gather.7
  231.9 72.1 all-gather.9
  307.5 55.5 all-gather.11
  366.6 59.5 all-gather.13
  430.0 74.4 reduce-scatter.1
